TPU v7x, 128 devices: a whole 4x4x4 slice. The times are simulated.
128 devices in a mesh: section: 2 (over y_lo), dp: 64 (over z, y_hi, x, core).
Axes of the slice: x: 4, y: 4 (y_hi: 2, y_lo: 2; y = y_hi * 2 + y_lo), z: 4, core: 2. Of those that a mesh axis runs over, the one named last changes fastest.
Arguments:
- hidden_in: bfloat16 [128, 128, 768], P('dp'), may hold values from -6 to 6
- cotangent: bfloat16 [128, 128, 768], P('dp'), may hold values from -6 to 6
- segment_ids: int32 [128, 128], P('dp'), may hold values from 0 to 3, never falling along the last dimension, each value on 1 to 64 neighbouring positions
- positions: int32 [128, 128], P('dp'), may hold values from 0 to 511, as said below
- w_in: bfloat16 [2, 768, 2304], P('section'), may hold values from -0.3125 to 0.3125
- b_in: bfloat16 [2, 2304], P('section'), may hold values from -1.1953125 to 1.1953125
- w_out: bfloat16 [2, 768, 768], P('section'), may hold values from -0.625 to 0.625
- w_up: bfloat16 [2, 768, 3072], P('section'), may hold values from -0.21875 to 0.21875
- b_up: bfloat16 [2, 3072], P('section'), may hold values from -1.1953125 to 1.1953125
- w_down: bfloat16 [2, 3072, 768], P('section'), may hold values from -0.15625 to 0.15625
- gains: bfloat16 [2, 2, 768], P('section'), may hold values from 0.5 to 1.5
- biases: bfloat16 [2, 4, 768], P('section'), may hold values from -1.1953125 to 1.1953125
- rel_table: bfloat16 [512, 768], replicated, may hold values from -6 to 6
- abs_table: bfloat16 [512, 768], replicated, may hold values from -3 to 3
Outputs:
- section_out: bfloat16 [2, 128, 128, 768], P('section', 'dp')
- input_grad: bfloat16 [2, 128, 128, 768], P('section', 'dp')
- g_w_in: float32 [2, 768, 2304], P('section')
- g_b_in: float32 [2, 2304], P('section')
- g_w_out: float32 [2, 768, 768], P('section')
- g_w_up: float32 [2, 768, 3072], P('section')
- g_b_up: float32 [2, 3072], P('section')
- g_w_down: float32 [2, 3072, 768], P('section')
- g_gains: float32 [2, 2, 768], P('section')
- g_biases: float32 [2, 4, 768], P('section')
- g_rel_table: float32 [512, 768], replicated
- g_abs_table: float32 [512, 768], replicated
Inputs may be any that keep to these rules, and one draw needn't show every extreme that they name: Each row holds 128 consecutive positions from a start of its own; one row ends at 511. `segment_ids`: ids never fall along a row; a document holds at most 64 tokens.
All inputs are finite; a program needn't handle non-finite values.
Results may differ from a plain program's by a relative error of at most 0.035.
The roundings to bfloat16 on the way count: a program that leaves them out, or rounds other values in their place, can miss the bound.
Values may be sent and summed in bfloat16 or wider, within the bound.
No kernel may reach another device: no remote copies, remote signals or barrier semaphores. Data moves between devices by JAX's collectives and lax.ppermute only.
A program may use at most 256 MiB of HBM per device.

v0:
```python
from functools import partial
import math

import jax
import jax.numpy as jnp
from jax import lax
from jax.sharding import PartitionSpec as P

HEADS = 12


norm_eps = 1e-06
negative = -1e30
highest_precision = lax.Precision.HIGHEST


def from_behind(value, axis, by):
    peers = lax.axis_size(axis)
    pairs = [(i, i + by) for i in range(peers) if 0 <= i + by < peers]
    return lax.ppermute(value, axis, pairs)


def matmul(left, right):
    return jnp.dot(left, right, preferred_element_type=jnp.float32)


def exact_dot(left, right):
    return jnp.dot(left, right, precision=highest_precision, preferred_element_type=jnp.float32)


def layer_norm(value, gain, shift):
    centered = value - jnp.mean(value, axis=-1, keepdims=True)
    spread = jnp.mean(centered * centered, axis=-1, keepdims=True)
    return centered * lax.rsqrt(spread + norm_eps) * gain + shift


def split_heads(value):
    return value.reshape(value.shape[0], HEADS, value.shape[1] // HEADS)


def skew_rows(table):
    head_count, length, width = table.shape
    flat = table.reshape(head_count, length * width)[:, length:]
    return flat.reshape(head_count, length, width - 1)[:, :, :length]


def unskew_rows(grid):
    head_count = grid.shape[0]
    length = grid.shape[1]
    padded = jnp.pad(grid, ((0, 0), (0, 0), (0, length - 1)))
    flat = jnp.pad(padded.reshape(head_count, length * (2 * length - 1)), ((0, 0), (length, 0)))
    return flat.reshape(head_count, length, 2 * length)


def masked_scores(
    query_head_split, key_head_split, relative_query, relative_key, same_doc, score_scale
):
    content = jnp.einsum(
        "ihd,jhd->hij", query_head_split, key_head_split, preferred_element_type=jnp.float32
    )
    distant_content_position = jnp.einsum(
        "ywt,nwt->wyn", query_head_split, relative_key, preferred_element_type=jnp.float32
    )
    distant_position_content = jnp.einsum(
        "ntr,ctr->tnc", key_head_split, relative_query, preferred_element_type=jnp.float32
    )
    summed = (
        content
        + skew_rows(distant_content_position)
        + jnp.swapaxes(skew_rows(distant_position_content), 1, 2)
    )
    return jnp.where(same_doc, summed * score_scale, negative)


def forward(inputs, extra_rows, segment, weights, relative_query, relative_key, score_scale):
    w_in, b_in, w_out, w_up, b_up, w_down, gains, biases = weights
    model_width = inputs.shape[1]
    gains_float = gains.astype(jnp.float32)
    biases_float = biases.astype(jnp.float32)
    start_rows = inputs.astype(jnp.float32) + extra_rows
    query_in = start_rows.astype(jnp.bfloat16)
    queries = (
        matmul(query_in, w_in[:, :model_width]) + b_in[:model_width].astype(jnp.float32)
    ).astype(jnp.bfloat16)
    key_value = (
        matmul(inputs, w_in[:, model_width:]) + b_in[model_width:].astype(jnp.float32)
    ).astype(jnp.bfloat16)
    same_doc = (segment[:, None] == segment[None, :])[None]
    scores = masked_scores(
        split_heads(queries),
        split_heads(key_value[:, :model_width]),
        relative_query,
        relative_key,
        same_doc,
        score_scale,
    )
    row_max = jnp.max(scores, axis=2, keepdims=True)
    exponent = jnp.exp(scores - row_max)
    row_total = jnp.sum(exponent, axis=2, keepdims=True)
    attn_probs = (exponent / row_total).astype(jnp.bfloat16)
    log_total = row_max + jnp.log(row_total)
    context = jnp.einsum(
        "hij,jhd->ihd",
        attn_probs,
        split_heads(key_value[:, model_width:]),
        preferred_element_type=jnp.float32,
    )
    context = context.reshape(inputs.shape[0], model_width).astype(jnp.bfloat16)
    resid_one = start_rows + matmul(context, w_out) + biases_float[0]
    hidden = layer_norm(resid_one, gains_float[0], biases_float[1])
    hidden_low = hidden.astype(jnp.bfloat16)
    gate_pre = matmul(hidden_low, w_up) + b_up.astype(jnp.float32)
    active = jax.nn.gelu(gate_pre, approximate=False).astype(jnp.bfloat16)
    resid_two = hidden + matmul(active, w_down) + biases_float[2]
    output = layer_norm(resid_two, gains_float[1], biases_float[3])
    return (
        output,
        (
            query_in,
            queries,
            key_value,
            same_doc,
            log_total,
            context,
            resid_one,
            hidden_low,
            gate_pre,
            active,
            resid_two,
        ),
    )


def backward_ffn(grad_out, saved_state, weights):
    w_in, b_in, w_out, w_up, b_up, w_down, gains, biases = weights
    resid_one, hidden_low, gate_pre, active, resid_two = saved_state[6:]
    gains_float = gains.astype(jnp.float32)
    biases_float = biases.astype(jnp.float32)
    unused_two, norm_two_back = jax.vjp(layer_norm, resid_two, gains_float[1], biases_float[3])
    d_resid_two, d_gain_two, d_shift_two = norm_two_back(grad_out)
    d_down = d_resid_two.astype(jnp.bfloat16)
    d_w_down = matmul(active.T, d_down)
    d_active = matmul(d_down, w_down.T)
    unused_gate, gelu_back = jax.vjp(partial(jax.nn.gelu, approximate=False), gate_pre)
    d_gate = gelu_back(d_active)[0].astype(jnp.bfloat16)
    d_w_up = matmul(hidden_low.T, d_gate)
    d_hidden = d_resid_two + matmul(d_gate, w_up.T)
    unused_one, norm_one_back = jax.vjp(layer_norm, resid_one, gains_float[0], biases_float[1])
    d_resid_one, d_gain_one, d_shift_one = norm_one_back(d_hidden)
    ffn_grads = (d_w_up, jnp.sum(d_gate.astype(jnp.float32), axis=0), d_w_down)
    d_gains = jnp.stack([d_gain_one, d_gain_two])
    norm_rows = (d_shift_one, jnp.sum(d_down.astype(jnp.float32), axis=0), d_shift_two)
    return (d_resid_one, ffn_grads, d_gains, norm_rows)


def backward_attention(
    d_resid_one, inputs, saved_state, weights, relative_query, relative_key, score_scale
):
    w_in, b_in, w_out = weights[:3]
    query_in, queries, key_value, same_doc, log_total, context = saved_state[:6]
    length, model_width = inputs.shape
    d_attended = d_resid_one.astype(jnp.bfloat16)
    d_w_out = matmul(context.T, d_attended)
    d_context = split_heads(matmul(d_attended, w_out.T).astype(jnp.bfloat16))
    query_head_split = split_heads(queries)
    key_head_split = split_heads(key_value[:, :model_width])
    v_heads = split_heads(key_value[:, model_width:])
    scores = masked_scores(
        query_head_split, key_head_split, relative_query, relative_key, same_doc, score_scale
    )
    attn_probs = jnp.exp(scores - log_total)
    d_probs = jnp.einsum("ihd,jhd->hij", d_context, v_heads, preferred_element_type=jnp.float32)
    d_value = jnp.einsum(
        "hij,ihd->jhd",
        attn_probs.astype(jnp.bfloat16),
        d_context,
        preferred_element_type=jnp.float32,
    )
    d_scores = (
        attn_probs * (d_probs - jnp.sum(d_probs * attn_probs, axis=2, keepdims=True))
    ).astype(jnp.bfloat16)
    distant_content_position_gradient = (
        score_scale * unskew_rows(d_scores).astype(jnp.float32)
    ).astype(jnp.bfloat16)
    distant_position_content_gradient = (
        score_scale * unskew_rows(jnp.swapaxes(d_scores, 1, 2)).astype(jnp.float32)
    ).astype(jnp.bfloat16)
    d_query = score_scale * jnp.einsum(
        "hij,jhd->ihd", d_scores, key_head_split, preferred_element_type=jnp.float32
    )
    d_query = d_query + jnp.einsum(
        "owg,goc->woc",
        distant_content_position_gradient,
        relative_key,
        preferred_element_type=jnp.float32,
    )
    key_gradient_rows = score_scale * jnp.einsum(
        "hij,ihd->jhd", d_scores, query_head_split, preferred_element_type=jnp.float32
    )
    key_gradient_rows = key_gradient_rows + jnp.einsum(
        "qol,lqc->oqc",
        distant_position_content_gradient,
        relative_query,
        preferred_element_type=jnp.float32,
    )
    table_rows = relative_key.shape[0]
    d_rel_k = jnp.einsum(
        "oba,bor->aor",
        distant_content_position_gradient,
        query_head_split,
        preferred_element_type=jnp.float32,
    ).reshape(table_rows, model_width)
    d_rel_q = jnp.einsum(
        "kay,ake->yke",
        distant_position_content_gradient,
        key_head_split,
        preferred_element_type=jnp.float32,
    ).reshape(table_rows, model_width)
    d_query = d_query.reshape(length, model_width).astype(jnp.bfloat16)
    d_key_value = jnp.concatenate(
        [key_gradient_rows.reshape(length, model_width), d_value.reshape(length, model_width)],
        axis=1,
    ).astype(jnp.bfloat16)
    d_start = d_resid_one + matmul(d_query, w_in[:, :model_width].T)
    d_inputs = d_start + matmul(d_key_value, w_in[:, model_width:].T)
    d_w_in = jnp.concatenate([matmul(query_in.T, d_query), matmul(inputs.T, d_key_value)], axis=1)
    d_b_in = jnp.concatenate(
        [
            jnp.sum(d_query.astype(jnp.float32), axis=0),
            jnp.sum(d_key_value.astype(jnp.float32), axis=0),
        ]
    )
    attended_sum = jnp.sum(d_attended.astype(jnp.float32), axis=0)
    return (d_inputs, (d_w_in, d_b_in, d_w_out), attended_sum, d_rel_q, d_rel_k, d_start)


def per_device(
    hidden_in,
    cotangent,
    segment_ids,
    positions,
    w_in,
    b_in,
    w_out,
    w_up,
    b_up,
    w_down,
    gains,
    biases,
    rel_table,
    abs_table,
):
    weights = (w_in[0], b_in[0], w_out[0], w_up[0], b_up[0], w_down[0], gains[0], biases[0])
    micro_count, length, model_width = hidden_in.shape
    half_table = rel_table.shape[0] // 2
    score_scale = 1.0 / math.sqrt(3 * (model_width // HEADS))
    section_index = lax.axis_index("section")
    is_last = section_index == 1
    last_flag = is_last.astype(jnp.float32)
    select_at = lax.broadcasted_iota(jnp.int32, (2 * length, 2 * half_table), 0)
    table_at = lax.broadcasted_iota(jnp.int32, (2 * length, 2 * half_table), 1)
    select_rows = (
        jnp.clip(length - select_at, -half_table, half_table - 1) + half_table == table_at
    ).astype(jnp.bfloat16)
    rel_rows = matmul(select_rows, rel_table).astype(jnp.bfloat16)
    rel_proj = (
        matmul(rel_rows, w_in[0][:, : 2 * model_width])
        + b_in[0][: 2 * model_width].astype(jnp.float32)
    ).astype(jnp.bfloat16)
    relative_query = split_heads(rel_proj[:, :model_width])
    relative_key = split_heads(rel_proj[:, model_width:])
    table_index = lax.broadcasted_iota(jnp.int32, (1, abs_table.shape[0]), 1)

    def choose(late_value, early_value):
        return jnp.where(is_last, late_value, early_value)

    received = jnp.zeros((length, model_width), jnp.bfloat16)
    stored = []
    outputs = []
    for tick_index in range(micro_count + 1):
        micro_slot = jnp.clip(tick_index - section_index, 0, micro_count - 1)
        inputs = choose(received, hidden_in[min(tick_index, micro_count - 1)])
        segment = lax.dynamic_index_in_dim(segment_ids, micro_slot, 0, keepdims=False)
        place_ids = lax.dynamic_index_in_dim(positions, micro_slot, 0, keepdims=False)
        onehot = (place_ids[:, None] == table_index).astype(jnp.bfloat16)
        extra_rows = last_flag * matmul(onehot, abs_table)
        output, saved_state = forward(
            inputs, extra_rows, segment, weights, relative_query, relative_key, score_scale
        )
        sent_rows = output.astype(jnp.bfloat16)
        outputs.append(sent_rows)
        stored.append((inputs, extra_rows, segment, onehot, saved_state))
        if tick_index < micro_count:
            received = from_behind(sent_rows, "section", 1)
    ffn_sums = (
        jnp.zeros(w_up[0].shape, jnp.float32),
        jnp.zeros(b_up[0].shape, jnp.float32),
        jnp.zeros(w_down[0].shape, jnp.float32),
    )
    attn_sums = (
        jnp.zeros(w_in[0].shape, jnp.float32),
        jnp.zeros(b_in[0].shape, jnp.float32),
        jnp.zeros(w_out[0].shape, jnp.float32),
    )
    gain_sum = jnp.zeros(gains[0].shape, jnp.float32)
    bias_sum = jnp.zeros(biases[0].shape, jnp.float32)
    rel_q_sum = jnp.zeros((2 * length, model_width), jnp.float32)
    rel_k_sum = jnp.zeros((2 * length, model_width), jnp.float32)
    abs_sum = jnp.zeros(abs_table.shape, jnp.float32)
    received = jnp.zeros((length, model_width), jnp.bfloat16)
    returned = []
    for tick_index in range(micro_count + 1):
        late_entry = stored[min(tick_index + 1, micro_count)]
        early_entry = stored[max(tick_index - 1, 0)]
        inputs, extra_rows, segment, onehot, saved_state = jax.tree.map(
            choose, late_entry, early_entry
        )
        if tick_index < micro_count:
            own_grad = cotangent[tick_index]
        else:
            own_grad = jnp.zeros((length, model_width), jnp.bfloat16)
        grad_out = choose(own_grad, received).astype(jnp.float32)
        d_resid_one, ffn_grads, d_gains, norm_rows = backward_ffn(grad_out, saved_state, weights)
        ffn_sums = jax.tree.map(jnp.add, ffn_sums, ffn_grads)
        if tick_index == micro_count:
            ffn_total = ffn_sums
        d_inputs, attn_grads, attended_sum, d_rel_q, d_rel_k, d_start = backward_attention(
            d_resid_one, inputs, saved_state, weights, relative_query, relative_key, score_scale
        )
        attn_sums = jax.tree.map(jnp.add, attn_sums, attn_grads)
        gain_sum = gain_sum + d_gains
        bias_sum = bias_sum + jnp.stack([attended_sum, norm_rows[0], norm_rows[1], norm_rows[2]])
        rel_q_sum = rel_q_sum + d_rel_q
        rel_k_sum = rel_k_sum + d_rel_k
        abs_sum = abs_sum + last_flag * exact_dot(onehot.astype(jnp.float32).T, d_start)
        sent_back = d_inputs.astype(jnp.bfloat16)
        returned.append(sent_back)
        if tick_index < micro_count:
            received = from_behind(sent_back, "section", -1)
    rel_pair = jnp.concatenate([rel_q_sum, rel_k_sum], axis=1)
    d_rel_rows = exact_dot(rel_pair, w_in[0][:, : 2 * model_width].astype(jnp.float32).T)
    d_rel_table = exact_dot(select_rows.astype(jnp.float32).T, d_rel_rows)
    d_w_in = (
        attn_sums[0]
        .at[:, : 2 * model_width]
        .add(exact_dot(rel_rows.astype(jnp.float32).T, rel_pair))
    )
    d_b_in = attn_sums[1].at[: 2 * model_width].add(jnp.sum(rel_pair, axis=0))
    d_w_out = attn_sums[2]
    summed = lax.psum(
        (d_w_in, d_b_in, d_w_out, ffn_total[0], ffn_total[1], ffn_total[2], gain_sum, bias_sum),
        "dp",
    )
    rel_total, abs_total = lax.psum((d_rel_table, abs_sum), ("section", "dp"))
    section_out = jnp.stack(
        [choose(outputs[row_index + 1], outputs[row_index]) for row_index in range(micro_count)]
    )
    input_grad = jnp.stack(
        [choose(returned[row_index], returned[row_index + 1]) for row_index in range(micro_count)]
    )
    g_w_in, g_b_in, g_w_out, g_w_up, g_b_up, g_w_down, g_gains, g_biases = summed
    return (
        section_out[None],
        input_grad[None],
        g_w_in[None],
        g_b_in[None],
        g_w_out[None],
        g_w_up[None],
        g_b_up[None],
        g_w_down[None],
        g_gains[None],
        g_biases[None],
        rel_total,
        abs_total,
    )


def solution(mesh):
    in_specs = (
        P("dp", None, None),
        P("dp", None, None),
        P("dp", None),
        P("dp", None),
        P("section", None, None),
        P("section", None),
        P("section", None, None),
        P("section", None, None),
        P("section", None),
        P("section", None, None),
        P("section", None, None),
        P("section", None, None),
        P(),
        P(),
    )
    out_specs = (
        P("section", "dp", None, None),
        P("section", "dp", None, None),
        P("section", None, None),
        P("section", None),
        P("section", None, None),
        P("section", None, None),
        P("section", None),
        P("section", None, None),
        P("section", None, None),
        P("section", None, None),
        P(),
        P(),
    )
    return jax.shard_map(
        per_device, mesh=mesh, in_specs=in_specs, out_specs=out_specs, check_vma=False
    )
```

profile of v0, /device:TPU:1, one launch (start us, length us, event | category | flops | bytes accessed | tf_op | source)
XLA Modules:
  0.0 1366.7 jit_solution(18224747681762011080)
XLA Ops:
  20.8 2.6 fusion.36
  27.1 4.9 reshape.946
  34.1 2.3 copy.169
  39.7 4.9 reshape.949
  49.5 6.0 fusion.45
  57.3 4.0 collective-permute-start
  61.4 3.5 collective-permute-done
  75.7 4.9 reshape.956
  83.9 5.0 reshape.954
  91.0 2.3 copy.170
  97.4 16.8 %fusion.48 = (bf16[128,3072]{1,0:T(8,128)(2,1)S(1)}, f32[128,3072]{1,0:T(8,128)}) fusion(f32[3072]{0:T(1024)S(1)} %bitcast.649, bf16[1,768,3072]{2,1,0:T(8,128)(2,1)S(1)} %bitcast.473, f32[128,768]{1,0:T(8,128)S(1)} %get-tuple-element.174, f32[128]{0:T(128)S(1)} %add_rsqrt_fusion.3, f32[128]{0:T(128)S(1)} %broadcast_multiply_fusion.9, ...), kind=kOutput, calls=%fused_computation.63 | convolution fusion | flops 630423552 | bytes 7490560 | tf_op jit(solution)/shard_map/dot_general | solution.py:24
  116.4 4.1 collective-permute-start.1
  124.2 2.6 broadcast_select_fusion.6
  129.7 3.4 broadcast_select_fusion
  145.2 4.9 reshape.963
  153.5 4.9 reshape.969
  162.6 5.3 reshape.961
  170.0 2.3 copy.171
  182.6 5.0 reshape.967
  189.7 2.3 copy.172
  192.0 7.8 fusion.51
  204.7 5.5 convert_reduce_fusion.2
  210.3 2.4 multiply_reduce_fusion.5
  226.2 3.5 reshape.972
  234.3 2.6 convolution_add_fusion.21
  239.7 3.5 reshape.973
  250.3 3.0 fusion.265
  253.4 5.6 fusion.270
  258.9 5.1 fusion.206
  273.1 5.0 reshape.981
  281.4 5.0 reshape.993
  293.2 5.3 reshape.979
  300.6 2.3 copy.173
  306.2 5.0 reshape.991
  313.2 2.3 copy.174
  319.5 3.0 fusion.392
  322.7 2.6 fusion.118
  325.3 2.6 fusion.113
  328.7 6.8 convert_reduce_fusion.1
  339.9 2.3 convolution_convert_fusion.2
  349.8 3.5 reshape.984
  356.3 2.6 convolution_add_fusion.18
  360.8 5.3 fusion.268
  366.1 5.0 fusion.204
  373.2 3.5 reshape.985
  381.1 3.2 fusion.266
  392.8 5.5 convert_reduce_fusion
  411.0 3.5 reshape.996
  417.5 2.6 convolution_add_fusion.15
  424.1 3.5 reshape.997
  432.6 4.1 fusion.40
  439.0 3.0 fusion.272
  442.0 4.6 fusion
  446.7 3.4 copy.196
  450.1 2.3 copy-done.1
  455.6 13.0 add_bitcast_fusion.1
  470.5 9.8 fusion.2
  480.5 5.2 add_bitcast_fusion
  494.3 324.2 %all-reduce.13 = (f32[1,2304]{1,0:T(1,128)}, f32[1,3072]{1,0:T(1,128)}, f32[1,2,768]{2,1,0:T(2,128)}, f32[1,4,768]{2,1,0:T(4,128)}) all-reduce(f32[1,2304]{1,0:T(1,128)S(1)} %reshape_dynamic-update-slice_fusion, f32[1,3072]{1,0:T(1,128)S(1)} %bitcast.647, ...), channel_id=1, replica_groups=mesh['section'=2,'dp'=64] {'dp'}, use_global_device_ids=true, to_apply=%region_54.55 | all-reduce | flops 9984 | bytes 79872 | tf_op jit(solution)/shard_map/psum | solution.py:350
  818.5 2.6 fusion.195
  821.9 513.5 %all-reduce.20.cloned.1.call-done = (f32[1,768,2304]{2,1,0:T(8,128)}, f32[1,768,768]{2,1,0:T(8,128)}, f32[1,768,3072]{2,1,0:T(8,128)}, f32[1,3072,768]{2,1,0:T(8,128)}) async-done(((f32[1,768,2304]{2,1,0:T(8,128)}, f32[1,768,768]{2,1,0:T(8,128)}, f32[1,768,3072]{2,1,0:T(8,128)}, f32[1,3072,768]{2,1,0:T(8,128)}), (f32[1,768,2304]{2,1,0:T(8,128)}, f32[1,768,768]{2,1,0:T(8,128)}, f32[1,768,3072]{2,1,0:T(8,128)}, ...) | async-done | bytes 28311568 | tf_op jit(solution)/shard_map/psum | solution.py:350
  1335.4 6.6 copy.204
  1343.4 9.3 copy.206
  1352.7 3.7 copy.207
  (828 shorter events, 232.0 us)
Async XLA Ops:
  7.2 41.5 %copy-start = (bf16[1,768,768]{2,1,0:T(8,128)(2,1)S(1)}, bf16[1,768,768]{2,1,0:T(8,128)(2,1)}, u32[]{:S(2)}) copy-start(bf16[1,768,768]{2,1,0:T(8,128)(2,1)} %param.24) | copy-start | bytes 3538948
  7.2 814.7 %all-reduce.18.cloned.1.call-start = ((), (), s32[]{:S(2)}) async-start(), calls=%async_computation | async-start | bytes 6291456 | tf_op jit(solution)/shard_map/psum | solution.py:354
  7.3 13.1 copy-start.203
  8.0 58.0 %copy-start.169 = (f32[768]{0:T(1024)}, f32[768]{0:T(1024)S(1)}, u32[]{:S(2)}) copy-start(f32[768]{0:T(1024)S(1)} %convert_reduce_fusion.20) | copy-start | bytes 9220
  14.5 34.2 %copy-start.10 = (f32[128,768]{1,0:T(8,128)}, f32[128,768]{1,0:T(8,128)S(1)}, u32[]{:S(2)}) copy-start(f32[128,768]{1,0:T(8,128)S(1)} %fusion.154) | copy-start | bytes 1179652
  38.2 11.2 slice-start.16
  44.7 70.7 %copy-start.156 = (f32[768]{0:T(1024)}, f32[768]{0:T(1024)S(1)}, u32[]{:S(2)}) copy-start(f32[768]{0:T(1024)S(1)} %get-tuple-element.53) | copy-start | bytes 9220
  55.5 9.4 copy-start.26
  55.5 9.4 copy-start.84
  55.5 9.4 copy-start.189
  56.5 9.5 copy-start.197
  56.7 11.6 copy-start.205
  57.3 7.6 collective-permute-start
  66.0 30.6 %copy-start.68 = (bf16[128,768]{1,0:T(8,128)(2,1)}, bf16[128,768]{1,0:T(8,128)(2,1)S(1)}, u32[]{:S(2)}) copy-start(bf16[128,768]{1,0:T(8,128)(2,1)S(1)} %get-tuple-element.113) | copy-start | bytes 589828
  83.9 13.4 slice-start.18
  96.6 17.6 %slice-start.8 = ((s8[4718592]{0:T(1024)(128)(4,1)}), s8[4194304]{0:T(1024)(128)(4,1)S(1)}, s32[]{:S(2)}) async-start(s8[4718592]{0:T(1024)(128)(4,1)} %bitcast.462), calls=%async_computation.10 | async-start | bytes 8388608
  97.1 17.1 %copy-start.175 = (f32[128]{0:T(128)}, f32[128]{0:T(128)S(1)}, u32[]{:S(2)}) copy-start(f32[128]{0:T(128)S(1)} %broadcast_multiply_fusion.9) | copy-start | bytes 1540
  97.4 16.8 %copy-start.194 = (f32[128]{0:T(128)}, f32[128]{0:T(128)S(1)}, u32[]{:S(2)}) copy-start(f32[128]{0:T(128)S(1)} %add_rsqrt_fusion.3) | copy-start | bytes 1540
  97.4 16.8 %slice-start.9 = ((s8[4718592]{0:T(1024)(128)(4,1)}), s8[524288]{0:T(1024)(128)(4,1)S(1)}, s32[]{:S(2)}) async-start(s8[4718592]{0:T(1024)(128)(4,1)} %bitcast.462), calls=%async_computation.11 | async-start | bytes 1048576
  115.1 9.0 copy-start.31
  115.5 8.7 copy-start.137
  115.5 8.7 copy-start.149
  115.5 8.7 copy-start.170
  116.4 10.4 copy-start.139
  116.4 6.7 collective-permute-start.1
  124.2 52.0 %copy-start.71 = (bf16[128,768]{1,0:T(8,128)(2,1)}, bf16[128,768]{1,0:T(8,128)(2,1)S(1)}, u32[]{:S(2)}) copy-start(bf16[128,768]{1,0:T(8,128)(2,1)S(1)} %get-tuple-element.111) | copy-start | bytes 589828
  127.9 50.8 %copy-start.48 = (bf16[128,768]{0,1:T(8,128)(2,1)}, bf16[128,768]{0,1:T(8,128)(2,1)S(1)}, u32[]{:S(2)}) copy-start(bf16[128,768]{0,1:T(8,128)(2,1)S(1)} %copy.125) | copy-start | bytes 589828
  182.6 17.1 %slice-start.10 = ((s8[4718592]{0:T(1024)(128)(4,1)}), s8[524288]{0:T(1024)(128)(4,1)S(1)}, s32[]{:S(2)}) async-start(s8[4718592]{0:T(1024)(128)(4,1)} %bitcast.464), calls=%async_computation.12 | async-start | bytes 1048576
  201.1 9.1 slice-start.20
  306.2 16.5 %copy-start.159 = (pred[128,128]{0,1:T(8,128)(4,1)S(1)}, pred[128,128]{0,1:T(8,128)(4,1)}, u32[]{:S(2)}) copy-start(pred[128,128]{0,1:T(8,128)(4,1)} %get-tuple-element.158) | copy-start | bytes 49156
  306.2 19.1 %copy-start.158 = (pred[128,128]{0,1:T(8,128)(4,1)S(1)}, pred[128,128]{0,1:T(8,128)(4,1)}, u32[]{:S(2)}) copy-start(pred[128,128]{0,1:T(8,128)(4,1)} %get-tuple-element.156) | copy-start | bytes 49156
  313.2 15.4 %slice-start.12 = ((s8[4718592]{0:T(1024)(128)(4,1)}), s8[524288]{0:T(1024)(128)(4,1)S(1)}, s32[]{:S(2)}) async-start(s8[4718592]{0:T(1024)(128)(4,1)} %bitcast.466), calls=%async_computation.14 | async-start | bytes 1048576
  316.9 11.1 copy-start.124
  318.2 9.8 collective-permute-start.2
  325.3 10.1 slice-start.22
  381.1 11.7 slice-start.14
  385.7 6.4 collective-permute-start.3
  387.0 11.4 slice-start.24
  430.4 8.5 copy-start.99
  430.4 8.5 copy-start.70
  430.5 8.5 copy-start.73
  430.5 11.5 slice-start.28
  432.6 9.4 slice-start.26
  432.6 9.4 slice-start.29
  454.6 14.0 %copy-start.103 = (bf16[128,768]{1,0:T(8,128)(2,1)S(1)}, bf16[128,768]{1,0:T(8,128)(2,1)}, u32[]{:S(2)}) copy-start(bf16[128,768]{1,0:T(8,128)(2,1)} %copy-done.102) | copy-start | bytes 589828
  454.7 14.0 %copy-start.152 = (bf16[12,64,128]{2,1,0:T(8,128)(2,1)S(1)}, bf16[12,64,128]{2,1,0:T(8,128)(2,1)}, u32[]{:S(2)}) copy-start(bf16[12,64,128]{2,1,0:T(8,128)(2,1)} %get-tuple-element.141) | copy-start | bytes 589828
  454.7 880.7 %all-reduce.20.cloned.1.call-start = ((), (), s32[]{:S(2)}) async-start(), calls=%async_computation.1 | async-start | bytes 56623104 | tf_op jit(solution)/shard_map/psum | solution.py:350
  455.5 13.1 copy-start.20
  455.5 13.1 copy-start.21
  455.6 15.0 %copy-start.23 = (f32[12,64,256]{2,1,0:T(8,128)S(1)}, f32[12,64,256]{2,1,0:T(8,128)}, u32[]{:S(2)}) copy-start(f32[12,64,256]{2,1,0:T(8,128)} %convolution_add_fusion.4) | copy-start | bytes 2359300
  455.6 24.8 %slice-start.3 = ((s8[9437184]{0:T(1024)(128)(4,1)}), s8[4194304]{0:T(1024)(128)(4,1)S(1)}, s32[]{:S(2)}) async-start(s8[9437184]{0:T(1024)(128)(4,1)} %bitcast.457), calls=%async_computation.5 | async-start | bytes 8388608
  455.6 24.8 %slice-start.4 = ((s8[9437184]{0:T(1024)(128)(4,1)}), s8[4194304]{0:T(1024)(128)(4,1)S(1)}, s32[]{:S(2)}) async-start(s8[9437184]{0:T(1024)(128)(4,1)} %bitcast.457), calls=%async_computation.6 | async-start | bytes 8388608
  468.6 11.8 slice-start
  468.6 11.8 slice-start.1
  468.6 11.8 slice-start.5
  470.5 9.9 slice-start.2
  470.5 9.9 copy-start.15
  470.5 9.9 copy-start.18
  470.5 9.9 copy-start.131
  490.2 328.3 %copy-start.97 = (bf16[12,64,128]{2,1,0:T(8,128)(2,1)S(1)}, bf16[12,64,128]{2,1,0:T(8,128)(2,1)}, u32[]{:S(2)}) copy-start(bf16[12,64,128]{2,1,0:T(8,128)(2,1)} %convolution_convert_fusion.1) | copy-start | bytes 589828
  490.2 328.3 %copy-start.100 = (bf16[12,64,128]{2,1,0:T(8,128)(2,1)S(1)}, bf16[12,64,128]{2,1,0:T(8,128)(2,1)}, u32[]{:S(2)}) copy-start(bf16[12,64,128]{2,1,0:T(8,128)(2,1)} %copy-done.99) | copy-start | bytes 589828
  1342.0 10.7 slice-start.30
  1343.4 9.3 slice-start.31
  1343.4 9.3 slice-start.32
  (200 other events, 667.0 us)
Sparse Core Ops, SparseCore 0:
  454.8 158.3 all-reduce.17
  616.7 718.6 all-reduce.19
where the time goes:
time: 1370 us
  waiting for transfers between devices  520 us (38%)
  blocking collectives  324 us (24%)
  matrix products  227 us (17%)
  local copies, waits for them, and re-layouts  224 us (16%)
  other arithmetic  43.5 us (3%)
  between operations  17.8 us (1%)
    psum x1, waiting for transfers between devices, per_device(): lax.psum((d_w_in, d_b_in, d_w_out, ffn_total[0], ffn_total[1], ffn_total[...  513 us
    psum x1, blocking collectives, per_device(): lax.psum((d_w_in, d_b_in, d_w_out, ffn_total[0], ffn_total[1], ffn_total[...  324 us
    dot_general x50, matrix products, matmul(): return jnp.dot(left, right, preferred_element_type=jnp.float32)  155 us
    unnamed x562, local copies, waits for them, and re-layouts  80.8 us
    reshape x12, local copies, waits for them, and re-layouts, skew_rows(): return flat.reshape(head_count, length, width - 1)[:, :, :length]  60.2 us
  transfers between devices with their start and end apart: 6, of which 4 were waited for; matrix products, arithmetic and copies ran while one was open for 4% of the time, Pallas kernels for 0%

commit v1 on v0

--- a/solution.py
+++ b/solution.py
@@ -18,6 +18,122 @@
     peers = lax.axis_size(axis)
     pairs = [(i, i + by) for i in range(peers) if 0 <= i + by < peers]
     return lax.ppermute(value, axis, pairs)
+
+
+SQUARE = ((0, 0), (1, 0), (1, 1), (0, 1))
+ROTATION = ("x0", "z0", "x1", "z1", "y")
+COLUMN_BLOCK = 768
+PIECES = 5
+
+
+def dp_place(index):
+    return {"core": index % 2, "x": index // 2 % 4, "y": index // 8 % 2, "z": index // 16}
+
+
+def dp_index(place):
+    return ((place["z"] * 2 + place["y"]) * 4 + place["x"]) * 2 + place["core"]
+
+
+def partner(index, dim):
+    place = dp_place(index)
+    if len(dim) == 2:
+        bits = list(SQUARE[place[dim[0]]])
+        bits[int(dim[1])] ^= 1
+        place[dim[0]] = SQUARE.index(tuple(bits))
+    else:
+        place[dim] ^= 1
+    return dp_index(place)
+
+
+def swap(value, dim):
+    peers = lax.axis_size("dp")
+    return lax.ppermute(value, "dp", [(i, partner(i, dim)) for i in range(peers)])
+
+
+def side(dim):
+    place = dp_place(lax.axis_index("dp"))
+    if len(dim) == 1 or dim == "core":
+        return place[dim].astype(jnp.int32)
+    at = place[dim[0]]
+    if dim[1] == "0":
+        return ((at == 1) | (at == 2)).astype(jnp.int32)
+    return (at >= 2).astype(jnp.int32)
+
+
+def order_of(piece):
+    return [ROTATION[(piece + step) % len(ROTATION)] for step in range(len(ROTATION))]
+
+
+def scatter_sums(pieces, orders):
+    for step in range(len(ROTATION)):
+        summed = []
+        for piece, order in zip(pieces, orders):
+            at, half = side(order[step]), piece.shape[0] // 2
+            sent = lax.dynamic_slice_in_dim(piece, (1 - at) * half, half, 0)
+            summed.append((piece, at, half, swap(sent, order[step])))
+        pieces = [
+            lax.dynamic_slice_in_dim(piece, at * half, half, 0) + received
+            for piece, at, half, received in summed
+        ]
+    return pieces
+
+
+def in_order(at, own, other, axis):
+    return jnp.where(
+        at == 0,
+        jnp.concatenate([own, other], axis=axis),
+        jnp.concatenate([other, own], axis=axis),
+    )
+
+
+def gather_pieces(pieces, orders):
+    for step in reversed(range(len(ROTATION))):
+        received = [swap(piece, order[step]) for piece, order in zip(pieces, orders)]
+        pieces = [
+            in_order(side(order[step]), piece, other, 0)
+            for piece, other, order in zip(pieces, received, orders)
+        ]
+    return pieces
+
+
+def cut_columns(value):
+    rows, width = value.shape
+    return [value[:, at : at + COLUMN_BLOCK] for at in range(0, width, COLUMN_BLOCK)]
+
+
+def cut_rows(value):
+    return [value[at : at + COLUMN_BLOCK] for at in range(0, value.shape[0], COLUMN_BLOCK)]
+
+
+def core_sum(blocks):
+    core = side("core")
+    half = COLUMN_BLOCK // 2
+    low = jnp.concatenate([block.astype(jnp.bfloat16) for block in blocks], axis=0)
+    own = lax.dynamic_slice_in_dim(low, core * half, half, 1)
+    other = lax.dynamic_slice_in_dim(low, (1 - core) * half, half, 1)
+    return own + swap(other, "core")
+
+
+def sum_over_rows(ffn_blocks, attn_blocks, tables, vectors):
+    table_rows = tables.shape[0]
+    rest = 1024 - table_rows - vectors.shape[0]
+    tail = jnp.pad(jnp.concatenate([tables, vectors], axis=0), ((0, rest), (0, 0)))
+    held = core_sum(ffn_blocks + attn_blocks + [tail])
+    size = held.shape[0] // PIECES
+    pieces = [held[at * size : (at + 1) * size] for at in range(PIECES)]
+    orders = [order_of(piece) for piece in range(PIECES)]
+    pieces = scatter_sums(pieces, orders)
+    first_row, span = 0, size
+    for dim in orders[-1]:
+        span //= 2
+        first_row = first_row + side(dim) * span
+    row_at = first_row + lax.broadcasted_iota(jnp.int32, pieces[-1].shape, 0) - (size - 1024)
+    is_table = (row_at >= 0) & (row_at < table_rows)
+    elsewhere = lax.ppermute(pieces[-1], "section", [(0, 1), (1, 0)])
+    pieces[-1] = jnp.where(is_table, pieces[-1] + elsewhere, pieces[-1])
+    pieces = gather_pieces(pieces, orders)
+    held = jnp.concatenate(pieces, axis=0)
+    return in_order(side("core"), held, swap(held, "core"), 1)
 
 
 def matmul(left, right):
@@ -347,18 +463,37 @@
     )
     d_b_in = attn_sums[1].at[: 2 * model_width].add(jnp.sum(rel_pair, axis=0))
     d_w_out = attn_sums[2]
-    summed = lax.psum(
-        (d_w_in, d_b_in, d_w_out, ffn_total[0], ffn_total[1], ffn_total[2], gain_sum, bias_sum),
-        "dp",
-    )
-    rel_total, abs_total = lax.psum((d_rel_table, abs_sum), ("section", "dp"))
+    vectors = jnp.concatenate(
+        [d_b_in, ffn_total[1], gain_sum.reshape(-1), bias_sum.reshape(-1)]
+    ).reshape(-1, model_width)
+    rel_used = half_table - length
+    total = sum_over_rows(
+        cut_columns(ffn_total[0]) + cut_rows(ffn_total[2]),
+        cut_columns(d_w_in) + [d_w_out],
+        jnp.concatenate([d_rel_table[rel_used:], abs_sum], axis=0),
+        vectors,
+    ).astype(jnp.float32)
+    blocks = cut_rows(total[: 12 * COLUMN_BLOCK])
+    g_w_up = jnp.concatenate(blocks[:4], axis=1)
+    g_w_down = jnp.concatenate(blocks[4:8], axis=0)
+    g_w_in = jnp.concatenate(blocks[8:11], axis=1)
+    g_w_out = blocks[11]
+    tail = total[12 * COLUMN_BLOCK :]
+    table_rows = rel_table.shape[0] - rel_used
+    rel_total = jnp.pad(tail[:table_rows], ((rel_used, 0), (0, 0)))
+    abs_total = tail[table_rows : table_rows + abs_table.shape[0]]
+    flat = tail[table_rows + abs_table.shape[0] :][: vectors.shape[0]].reshape(-1)
+    ends = (b_in.shape[1], b_up.shape[1], 2 * model_width, 4 * model_width)
+    starts = [sum(ends[:at]) for at in range(4)]
+    g_b_in, g_b_up, g_gains, g_biases = [flat[at : at + n] for at, n in zip(starts, ends)]
+    g_gains = g_gains.reshape(2, model_width)
+    g_biases = g_biases.reshape(4, model_width)
     section_out = jnp.stack(
         [choose(outputs[row_index + 1], outputs[row_index]) for row_index in range(micro_count)]
     )
     input_grad = jnp.stack(
         [choose(returned[row_index], returned[row_index + 1]) for row_index in range(micro_count)]
     )
-    g_w_in, g_b_in, g_w_out, g_w_up, g_b_up, g_w_down, g_gains, g_biases = summed
     return (
         section_out[None],
         input_grad[None],

time: 1370 us -> 733 us (0.54)
  waiting for transfers between devices: 520 us -> 57.4 us
  blocking collectives: 324 us -> 0 us
  starting transfers between devices: 10.8 us -> 95.8 us
  other arithmetic: 43.5 us -> 97.5 us
  local copies, waits for them, and re-layouts: 224 us -> 257 us
  matrix products: 227 us -> 209 us
    psum x2 -> x0, waiting for transfers between devices: 513 us -> none  [the longest x1 513 us: per_device(): lax.psum((d_w_in, d_b_in, d_w_out, ffn_total[0], ffn_total[1], ffn_total[...]
    psum x1 -> x0, blocking collectives: 324 us -> none  [per_device(): lax.psum((d_w_in, d_b_in, d_w_out, ffn_total[0], ffn_total[1], ffn_total[...]
    ppermute x0 -> x53, starting transfers between devices: none -> 84.1 us  [the longest x52 83.2 us: swap(): lax.ppermute(value, 'dp', [(i, partner(i, dim)) for i in range(peers)])]
    ppermute x0 -> x53, waiting for transfers between devices: none -> 53.9 us  [the longest x52 53.9 us: swap(): lax.ppermute(value, 'dp', [(i, partner(i, dim)) for i in range(peers)])]
    convert_element_type x0 -> x1, other arithmetic: none -> 23.4 us  [per_device(): total = sum_over_rows(cut_columns(ffn_total[0]) + cut_rows(ffn_total[2]),...]
    slice x0 -> x7, local copies, waits for them, and re-layouts: none -> 14 us  [the longest x1 8.96 us: cut_rows(): value[at:at + COLUMN_BLOCK]]
    unnamed x562 -> x563, local copies, waits for them, and re-layouts: 80.8 us -> 67.1 us
  transfers between devices with their start and end apart: 6 -> 57, of which waited for: 4 -> 18; matrix products, arithmetic and copies ran while one was open for 4% -> 14% of each run, Pallas kernels for 0% -> 0%
where the time goes in v1:
time: 733 us; the launch traced here: 722 us
  local copies, waits for them, and re-layouts  257 us (35%)
  matrix products  209 us (29%)
  other arithmetic  97.5 us (13%)
  starting transfers between devices  95.8 us (13%)
  waiting for transfers between devices  57.4 us (8%)
    dot_general x50, matrix products, matmul(): return jnp.dot(left, right, preferred_element_type=jnp.float32)  143 us
    ppermute x52, starting transfers between devices, swap(): lax.ppermute(value, 'dp', [(i, partner(i, dim)) for i in range(peers)])  83.2 us
    unnamed x563, local copies, waits for them, and re-layouts  67.1 us
    reshape x12, local copies, waits for them, and re-layouts, skew_rows(): return flat.reshape(head_count, length, width - 1)[:, :, :length]  59.5 us
    ppermute x52, waiting for transfers between devices, swap(): lax.ppermute(value, 'dp', [(i, partner(i, dim)) for i in range(peers)])  53.9 us
    convert_element_type x1, other arithmetic, per_device(): total = sum_over_rows(cut_columns(ffn_total[0]) + cut_rows(ffn_total[2]),...  23.4 us
    reshape x6, local copies, waits for them, and re-layouts, unskew_rows(): padded.reshape(head_count, length * (2 * length - 1))  21.8 us
    dot_general x6, matrix products, exact_dot(): jnp.dot(left, right, precision=highest_precision, preferred_element_type=...  19.9 us
  transfers between devices with their start and end apart: 57, of which 18 were waited for; matrix products, arithmetic and copies ran while one was open for 14% of the time, Pallas kernels for 0%

profile of v1, /device:TPU:1, one launch (start us, length us, event | category | flops | bytes accessed | tf_op | source)
XLA Modules:
  0.0 721.8 jit_solution(5600131995481545457)
XLA Ops:
  14.6 4.9 reshape.973
  29.5 5.0 reshape.976
  39.3 6.0 fusion.49
  47.2 4.0 collective-permute-start
  51.2 3.5 collective-permute-done
  61.6 4.9 reshape.981
  77.4 5.0 reshape.983
  88.2 15.6 %fusion.52 = (bf16[128,3072]{1,0:T(8,128)(2,1)S(1)}, f32[128,3072]{1,0:T(8,128)}) fusion(f32[3072]{0:T(1024)S(1)} %bitcast.643, bf16[1,768,3072]{2,1,0:T(8,128)(2,1)S(1)} %bitcast.474, f32[128,768]{1,0:T(8,128)S(1)} %get-tuple-element.179, f32[128]{0:T(128)S(1)} %add_rsqrt_fusion.3, f32[128]{0:T(128)S(1)} %broadcast_multiply_fusion.9, ...), kind=kOutput, calls=%fused_computation.75 | convolution fusion | flops 630423552 | bytes 7490560 | tf_op jit(solution)/shard_map/dot_general | solution.py:140
  106.5 4.8 collective-permute-start.1
  116.4 2.6 broadcast_select_fusion.6
  125.0 4.9 reshape.988
  134.3 3.2 broadcast_select_fusion
  144.3 4.9 reshape.990
  157.3 5.4 fusion.55
  167.1 5.5 convert_reduce_fusion.2
  181.9 4.9 reshape.994
  197.4 4.9 reshape.996
  212.3 3.7 reshape.1000
  221.0 3.5 reshape.999
  233.0 2.9 fusion.279
  237.9 5.3 fusion.292
  243.2 5.1 fusion.220
  254.9 4.9 reshape.1006
  268.8 5.0 reshape.1008
  280.4 4.9 reshape.1018
  295.3 5.0 reshape.1020
  306.5 3.0 fusion.408
  313.0 2.6 fusion.126
  317.9 6.8 convert_reduce_fusion.1
  338.1 3.5 reshape.1012
  344.9 2.9 fusion.280
  348.8 3.5 reshape.1011
  358.4 5.3 fusion.290
  363.7 5.0 fusion.218
  379.8 3.3 fusion.315
  385.8 8.1 %convert_reduce_fusion = (f32[3072]{0:T(1024)}, bf16[128,3072]{1,0:T(8,128)(2,1)S(1)}) fusion(bf16[128,768]{1,0:T(8,128)(2,1)S(1)} %get-tuple-element.64, bf16[1,3072,768]{2,1,0:T(8,128)(2,1)} %param.27, f32[128,3072]{1,0:T(8,128)S(1)} %copy-done.230, f32[128,3072]{1,0:T(8,128)} %get-tuple-element.181, pred[]{:T(512)S(6)} %eq.254), kind=kOutput, calls=%fused_computation.109 | convolution fusion | flops 633467904 | bytes 8859649 | tf_op jit(solution)/shard_map/dot_general | solution.py:140
  403.0 3.5 reshape.1024
  410.2 3.9 reshape.1023
  419.7 3.9 fusion.44
  425.7 2.9 fusion.281
  434.7 8.1 %add_convert_fusion.1 = bf16[768,3072]{1,0:T(8,128)(2,1)S(1)} fusion(f32[768,3072]{1,0:T(8,128)} %fusion.292, f32[768,3072]{1,0:T(8,128)} %fusion.290, bf16[128,3072]{1,0:T(8,128)(2,1)S(1)} %copy-done.82, bf16[128,768]{1,0:T(8,128)(2,1)S(1)} %copy-done.90, pred[]{:T(512)S(6)} %eq.254, f32[128,768]{1,0:T(8,128)S(1)} %get-tuple-element.179, ...), kind=kOutput, calls=%fused_computation.5 | convolution fusion | flops 611647488 | bytes 24976384 | tf_op jit(solution)/shard_map/dot_general | solution.py:140
  447.4 11.7 %fusion.1 = f32[768,2304]{1,0:T(8,128)} fusion(f32[768,1536]{1,0:T(8,128)} %fusion.279, f32[768,768]{1,0:T(8,128)} %fusion.287, f32[768,1536]{1,0:T(8,128)} %fusion.280, f32[768,768]{1,0:T(8,128)} %fusion.285, f32[768,1536]{1,0:T(8,128)} %fusion.281, f32[768,768]{1,0:T(8,128)} %fusion.283), kind=kLoop, calls=%fused_computation.8 | loop fusion | flops 8847360 | bytes 28311552 | tf_op jit(solution)/shard_map/add | solution.py:446
  459.1 8.6 %fusion.3 = bf16[768,1536]{1,0:T(8,128)(2,1)} fusion(f32[768,2304]{1,0:T(8,128)} %fusion.1, bf16[256,768]{1,0:T(8,128)(2,1)} %copy-done.112, pred[]{:T(512)} %compare_reduce_fusion, f32[256,768]{0,1:T(8,128)} %bitcast.531, f32[256,768]{0,1:T(8,128)} %bitcast.528), kind=kOutput, calls=%fused_computation.12 | convolution fusion | flops 3627810816 | bytes 9043969 | tf_op jit(solution)/shard_map/dot_general | solution.py:144
  467.9 4.6 fusion.2
  476.1 3.2 fusion.177
  483.9 6.9 constant_dynamic-slice_fusion.25
  493.0 12.4 %collective-permute-done.4 = bf16[10240,384]{1,0:T(8,128)(2,1)} collective-permute-done((bf16[10240,384]{1,0:T(8,128)(2,1)}, bf16[10240,384]{1,0:T(8,128)(2,1)}, u32[]{:S(2)}, u32[]{:S(2)}) %collective-permute-start.4) | collective-permute-done | bytes 7864352 | tf_op jit(solution)/shard_map/ppermute | solution.py:50
  505.3 6.8 dynamic-slice_add_fusion
  516.5 2.6 collective-permute-start.45
  521.3 3.8 collective-permute-start.35
  529.3 7.8 %collective-permute-done.45 = bf16[1024,384]{1,0:T(8,128)(2,1)} collective-permute-done((bf16[1024,384]{1,0:T(8,128)(2,1)}, bf16[1024,384]{1,0:T(8,128)(2,1)}, u32[]{:S(2)}, u32[]{:S(2)}) %collective-permute-start.45) | collective-permute-done | bytes 786464 | tf_op jit(solution)/shard_map/ppermute | solution.py:50
  539.8 2.8 collective-permute-done.35
  550.7 4.8 collective-permute-done.46
  616.1 3.6 collective-permute-done.54
  632.4 4.2 collective-permute-done.55
  638.2 14.4 %collective-permute-start.56 = (bf16[10240,384]{1,0:T(8,128)(2,1)}, bf16[10240,384]{1,0:T(8,128)(2,1)}, u32[]{:S(2)}, u32[]{:S(2)}) collective-permute-start(bf16[10240,384]{1,0:T(8,128)(2,1)} %fusion.78), channel_id=1, source_target_pairs={{0,1},{1,0},{2,3},{3,2},{4,5},{5,4},{6,7},{7,6},{8,9},{9,8},{10,11... | collective-permute-start | bytes 23592968 | tf_op jit(solution)/shard_map/ppermute | solution.py:50
  654.5 2.6 fusion.209
  657.9 7.0 collective-permute-done.56
  664.9 23.4 %fusion = f32[10240,768]{1,0:T(8,128)} fusion(bf16[10240,384]{1,0:T(8,128)(2,1)} %collective-permute-done.56, bf16[10240,384]{1,0:T(8,128)(2,1)} %fusion.78, pred[]{:T(512)S(6)} %eq.280), kind=kLoop, calls=%fused_computation.1 | loop fusion | flops 78643200 | bytes 47185920 | tf_op jit(solution)/shard_map/convert_element_type | solution.py:475
  688.3 9.0 %fusion.372 = (f32[768,768]{1,0:T(8,128)S(1)}, f32[768,768]{1,0:T(8,128)S(1)}, f32[768,768]{1,0:T(8,128)S(1)}, f32[768,768]{1,0:T(8,128)S(1)}, f32[1,768,768]{2,...) fusion(f32[10240,768]{1,0:T(8,128)} %fusion), kind=kLoop, calls=%fused_computation.730 | loop fusion | bytes 37748736 | tf_op jit(solution)/shard_map/slice | solution.py:105
  697.2 8.0 %slice_bitcast_fusion = f32[1,3072,768]{2,1,0:T(8,128)} fusion(f32[10240,768]{1,0:T(8,128)} %fusion), kind=kLoop, calls=%fused_computation.2 | loop fusion | bytes 18874368 | tf_op jit(solution)/shard_map/broadcast_in_dim | solution.py:505
  705.3 2.7 slice.545
  714.0 3.2 maximum_bitcast_fusion.1
  717.2 4.2 maximum_bitcast_fusion
  (1022 shorter events, 361.2 us)
Async XLA Ops:
  0.6 37.8 %copy-start = (bf16[1,768,768]{2,1,0:T(8,128)(2,1)S(1)}, bf16[1,768,768]{2,1,0:T(8,128)(2,1)}, u32[]{:S(2)}) copy-start(bf16[1,768,768]{2,1,0:T(8,128)(2,1)} %param.24) | copy-start | bytes 3538948
  5.3 33.2 %copy-start.9 = (f32[128,768]{1,0:T(8,128)}, f32[128,768]{1,0:T(8,128)S(1)}, u32[]{:S(2)}) copy-start(f32[128,768]{1,0:T(8,128)S(1)} %fusion.167) | copy-start | bytes 1179652
  38.4 66.6 %copy-start.146 = (f32[768]{0:T(1024)}, f32[768]{0:T(1024)S(1)}, u32[]{:S(2)}) copy-start(f32[768]{0:T(1024)S(1)} %get-tuple-element.53) | copy-start | bytes 9220
  47.2 7.6 %collective-permute-start = (bf16[128,768]{1,0:T(8,128)(2,1)S(1)}, bf16[128,768]{1,0:T(8,128)(2,1)S(1)}, u32[]{:S(2)}, u32[]{:S(2)}) collective-permute-start(bf16[128,768]{1,0:T(8,128)(2,1)S(1)} %add_convert_fusion.5), channel_id=1, source_target_pairs={{0,64},{1,65},{2,66},{3,67},{4,68},{5,69},{6,70},{7,71},{8,72},{9,... | collective-permute-start | bytes 589832 | tf_op jit(solution)/shard_map/ppermute | solution.py:20
  55.8 31.6 %copy-start.68 = (bf16[128,768]{1,0:T(8,128)(2,1)}, bf16[128,768]{1,0:T(8,128)(2,1)S(1)}, u32[]{:S(2)}) copy-start(bf16[128,768]{1,0:T(8,128)(2,1)S(1)} %get-tuple-element.103) | copy-start | bytes 589828
  106.5 7.0 collective-permute-start.1
  115.7 39.7 %copy-start.71 = (bf16[128,768]{1,0:T(8,128)(2,1)}, bf16[128,768]{1,0:T(8,128)(2,1)S(1)}, u32[]{:S(2)}) copy-start(bf16[128,768]{1,0:T(8,128)(2,1)S(1)} %get-tuple-element.101) | copy-start | bytes 589828
  248.3 67.8 %collective-permute-start.2 = (bf16[128,768]{1,0:T(8,128)(2,1)}, bf16[128,768]{1,0:T(8,128)(2,1)}, u32[]{:S(2)}, u32[]{:S(2)}) collective-permute-start(bf16[128,768]{1,0:T(8,128)(2,1)} %fusion.205), channel_id=1, source_target_pairs={{64,0},{65,1},{66,2},{67,3},{68,4},{69,5},{70,6},{71,7},{72,8},{73... | collective-permute-start | bytes 589832 | tf_op jit(solution)/shard_map/ppermute | solution.py:20
  295.3 22.5 %slice-start.13 = ((s8[4718592]{0:T(1024)(128)(4,1)}), s8[524288]{0:T(1024)(128)(4,1)S(1)}, s32[]{:S(2)}) async-start(s8[4718592]{0:T(1024)(128)(4,1)} %bitcast.469), calls=%async_computation.13 | async-start | bytes 1048576
  371.8 11.4 %collective-permute-start.3 = (bf16[128,768]{1,0:T(8,128)(2,1)}, bf16[128,768]{1,0:T(8,128)(2,1)}, u32[]{:S(2)}, u32[]{:S(2)}) collective-permute-start(bf16[128,768]{1,0:T(8,128)(2,1)} %fusion.206), channel_id=1, source_target_pairs={{64,0},{65,1},{66,2},{67,3},{68,4},{69,5},{70,6},{71,7},{72,8},{73... | collective-permute-start | bytes 589832 | tf_op jit(solution)/shard_map/ppermute | solution.py:20
  445.1 22.7 %slice-start.1 = ((s8[9437184]{0:T(1024)(128)(4,1)}), s8[4194304]{0:T(1024)(128)(4,1)S(1)}, s32[]{:S(2)}) async-start(s8[9437184]{0:T(1024)(128)(4,1)} %bitcast.459), calls=%async_computation.1 | async-start | bytes 8388608
  490.8 14.5 %collective-permute-start.4 = (bf16[10240,384]{1,0:T(8,128)(2,1)}, bf16[10240,384]{1,0:T(8,128)(2,1)}, u32[]{:S(2)}, u32[]{:S(2)}) collective-permute-start(bf16[10240,384]{1,0:T(8,128)(2,1)} %constant_dynamic-slice_fusion.25), channel_id=1, source_target_pairs={{0,1},{1,0},{2,3},{3,2},{4,5},{5,4},{6,7},{7,6},{8,9},{9,8},{10,11... | collective-permute-start | bytes 23592968 | tf_op jit(solution)/shard_map/ppermute | solution.py:50
  516.5 20.5 %collective-permute-start.45 = (bf16[1024,384]{1,0:T(8,128)(2,1)}, bf16[1024,384]{1,0:T(8,128)(2,1)}, u32[]{:S(2)}, u32[]{:S(2)}) collective-permute-start(bf16[1024,384]{1,0:T(8,128)(2,1)} %constant_dynamic-slice_fusion.4), channel_id=1, source_target_pairs={{0,8},{1,9},{2,10},{3,11},{4,12},{5,13},{6,14},{7,15},{8,0},{9,1},... | collective-permute-start | bytes 2359304 | tf_op jit(solution)/shard_map/ppermute | solution.py:50
  521.3 21.3 %collective-permute-start.35 = (bf16[1024,384]{1,0:T(8,128)(2,1)}, bf16[1024,384]{1,0:T(8,128)(2,1)}, u32[]{:S(2)}, u32[]{:S(2)}) collective-permute-start(bf16[1024,384]{1,0:T(8,128)(2,1)} %constant_dynamic-slice_fusion.9), channel_id=1, source_target_pairs={{0,48},{1,49},{2,50},{3,51},{4,52},{5,53},{6,54},{7,55},{8,56},{9,... | collective-permute-start | bytes 2359304 | tf_op jit(solution)/shard_map/ppermute | solution.py:50
  526.4 19.4 %collective-permute-start.25 = (bf16[1024,384]{1,0:T(8,128)(2,1)S(1)}, bf16[1024,384]{1,0:T(8,128)(2,1)S(1)}, u32[]{:S(2)}, u32[]{:S(2)}) collective-permute-start(bf16[1024,384]{1,0:T(8,128)(2,1)S(1)} %constant_dynamic-slice_fusion.14), channel_id=1, source_target_pairs={{0,6},{1,7},{2,4},{3,5},{4,2},{5,3},{6,0},{7,1},{8,14},{9,15},{10,... | collective-permute-start | bytes 2359304 | tf_op jit(solution)/shard_map/ppermute | solution.py:50
  529.0 19.2 %collective-permute-start.15 = (bf16[1024,384]{1,0:T(8,128)(2,1)S(1)}, bf16[1024,384]{1,0:T(8,128)(2,1)S(1)}, u32[]{:S(2)}, u32[]{:S(2)}) collective-permute-start(bf16[1024,384]{1,0:T(8,128)(2,1)S(1)} %constant_dynamic-slice_fusion.19), channel_id=1, source_target_pairs={{0,16},{1,17},{2,18},{3,19},{4,20},{5,21},{6,22},{7,23},{8,24},{9,... | collective-permute-start | bytes 2359304 | tf_op jit(solution)/shard_map/ppermute | solution.py:50
  529.2 21.2 %collective-permute-start.5 = (bf16[1024,384]{1,0:T(8,128)(2,1)S(1)}, bf16[1024,384]{1,0:T(8,128)(2,1)S(1)}, u32[]{:S(2)}, u32[]{:S(2)}) collective-permute-start(bf16[1024,384]{1,0:T(8,128)(2,1)S(1)} %constant_dynamic-slice_fusion.24), channel_id=1, source_target_pairs={{0,2},{1,3},{2,0},{3,1},{4,6},{5,7},{6,4},{7,5},{8,10},{9,11},{10,... | collective-permute-start | bytes 2359304 | tf_op jit(solution)/shard_map/ppermute | solution.py:50
  538.5 17.0 %collective-permute-start.46 = (bf16[512,384]{1,0:T(8,128)(2,1)S(1)}, bf16[512,384]{1,0:T(8,128)(2,1)S(1)}, u32[]{:S(2)}, u32[]{:S(2)}) collective-permute-start(bf16[512,384]{1,0:T(8,128)(2,1)S(1)} %constant_dynamic-slice_fusion.3), channel_id=1, source_target_pairs={{0,2},{1,3},{2,0},{3,1},{4,6},{5,7},{6,4},{7,5},{8,10},{9,11},{10,... | collective-permute-start | bytes 1179656 | tf_op jit(solution)/shard_map/ppermute | solution.py:50
  544.0 12.9 %collective-permute-start.36 = (bf16[512,384]{1,0:T(8,128)(2,1)S(1)}, bf16[512,384]{1,0:T(8,128)(2,1)S(1)}, u32[]{:S(2)}, u32[]{:S(2)}) collective-permute-start(bf16[512,384]{1,0:T(8,128)(2,1)S(1)} %constant_dynamic-slice_fusion.8), channel_id=1, source_target_pairs={{0,8},{1,9},{2,10},{3,11},{4,12},{5,13},{6,14},{7,15},{8,0},{9,1},... | collective-permute-start | bytes 1179656 | tf_op jit(solution)/shard_map/ppermute | solution.py:50
  546.0 11.2 %collective-permute-start.26 = (bf16[512,384]{1,0:T(8,128)(2,1)S(1)}, bf16[512,384]{1,0:T(8,128)(2,1)S(1)}, u32[]{:S(2)}, u32[]{:S(2)}) collective-permute-start(bf16[512,384]{1,0:T(8,128)(2,1)S(1)} %constant_dynamic-slice_fusion.13), channel_id=1, source_target_pairs={{0,48},{1,49},{2,50},{3,51},{4,52},{5,53},{6,54},{7,55},{8,56},{9,... | collective-permute-start | bytes 1179656 | tf_op jit(solution)/shard_map/ppermute | solution.py:50
  548.5 9.8 %collective-permute-start.16 = (bf16[512,384]{1,0:T(8,128)(2,1)S(1)}, bf16[512,384]{1,0:T(8,128)(2,1)S(1)}, u32[]{:S(2)}, u32[]{:S(2)}) collective-permute-start(bf16[512,384]{1,0:T(8,128)(2,1)S(1)} %constant_dynamic-slice_fusion.18), channel_id=1, source_target_pairs={{0,6},{1,7},{2,4},{3,5},{4,2},{5,3},{6,0},{7,1},{8,14},{9,15},{10,... | collective-permute-start | bytes 1179656 | tf_op jit(solution)/shard_map/ppermute | solution.py:50
  550.6 9.7 %collective-permute-start.6 = (bf16[512,384]{1,0:T(8,128)(2,1)S(1)}, bf16[512,384]{1,0:T(8,128)(2,1)S(1)}, u32[]{:S(2)}, u32[]{:S(2)}) collective-permute-start(bf16[512,384]{1,0:T(8,128)(2,1)S(1)} %constant_dynamic-slice_fusion.23), channel_id=1, source_target_pairs={{0,16},{1,17},{2,18},{3,19},{4,20},{5,21},{6,22},{7,23},{8,24},{9,... | collective-permute-start | bytes 1179656 | tf_op jit(solution)/shard_map/ppermute | solution.py:50
  555.6 7.5 %collective-permute-start.47 = (bf16[256,384]{1,0:T(8,128)(2,1)S(1)}, bf16[256,384]{1,0:T(8,128)(2,1)S(1)}, u32[]{:S(2)}, u32[]{:S(2)}) collective-permute-start(bf16[256,384]{1,0:T(8,128)(2,1)S(1)} %constant_dynamic-slice_fusion.2), channel_id=1, source_target_pairs={{0,16},{1,17},{2,18},{3,19},{4,20},{5,21},{6,22},{7,23},{8,24},{9,... | collective-permute-start | bytes 589832 | tf_op jit(solution)/shard_map/ppermute | solution.py:50
  557.0 7.2 collective-permute-start.37
  557.3 7.3 %collective-permute-start.27 = (bf16[256,384]{1,0:T(8,128)(2,1)S(1)}, bf16[256,384]{1,0:T(8,128)(2,1)S(1)}, u32[]{:S(2)}, u32[]{:S(2)}) collective-permute-start(bf16[256,384]{1,0:T(8,128)(2,1)S(1)} %constant_dynamic-slice_fusion.12), channel_id=1, source_target_pairs={{0,8},{1,9},{2,10},{3,11},{4,12},{5,13},{6,14},{7,15},{8,0},{9,1},... | collective-permute-start | bytes 589832 | tf_op jit(solution)/shard_map/ppermute | solution.py:50
  558.4 6.6 collective-permute-start.17
  560.5 6.2 collective-permute-start.7
  563.3 4.8 collective-permute-start.48
  564.3 5.5 collective-permute-start.38
  564.8 7.6 %collective-permute-start.28 = (bf16[128,384]{1,0:T(8,128)(2,1)S(1)}, bf16[128,384]{1,0:T(8,128)(2,1)S(1)}, u32[]{:S(2)}, u32[]{:S(2)}) collective-permute-start(bf16[128,384]{1,0:T(8,128)(2,1)S(1)} %constant_dynamic-slice_fusion.11), channel_id=1, source_target_pairs={{0,2},{1,3},{2,0},{3,1},{4,6},{5,7},{6,4},{7,5},{8,10},{9,11},{10,... | collective-permute-start | bytes 294920 | tf_op jit(solution)/shard_map/ppermute | solution.py:50
  565.1 7.4 %collective-permute-start.18 = (bf16[128,384]{1,0:T(8,128)(2,1)S(1)}, bf16[128,384]{1,0:T(8,128)(2,1)S(1)}, u32[]{:S(2)}, u32[]{:S(2)}) collective-permute-start(bf16[128,384]{1,0:T(8,128)(2,1)S(1)} %constant_dynamic-slice_fusion.16), channel_id=1, source_target_pairs={{0,8},{1,9},{2,10},{3,11},{4,12},{5,13},{6,14},{7,15},{8,0},{9,1},... | collective-permute-start | bytes 294920 | tf_op jit(solution)/shard_map/ppermute | solution.py:50
  566.9 6.7 collective-permute-start.8
  568.1 6.6 collective-permute-start.49
  569.9 5.7 collective-permute-start.39
  572.4 4.6 collective-permute-start.29
  572.6 5.7 collective-permute-start.19
  573.6 4.8 collective-permute-start.9
  574.7 6.0 collective-permute-start.50
  575.6 6.3 collective-permute-start.40
  577.0 5.0 collective-permute-start.30
  578.3 4.9 collective-permute-start.20
  578.4 5.9 collective-permute-start.10
  580.8 5.4 collective-permute-start.51
  581.9 9.1 %collective-permute-start.41 = (bf16[128,384]{1,0:T(8,128)(2,1)S(1)}, bf16[128,384]{1,0:T(8,128)(2,1)S(1)}, u32[]{:S(2)}, u32[]{:S(2)}) collective-permute-start(bf16[128,384]{1,0:T(8,128)(2,1)S(1)} %maximum_select_fusion.24), channel_id=1, source_target_pairs={{0,16},{1,17},{2,18},{3,19},{4,20},{5,21},{6,22},{7,23},{8,24},{9,... | collective-permute-start | bytes 294920 | tf_op jit(solution)/shard_map/ppermute | solution.py:50
  582.1 13.3 %collective-permute-start.31 = (bf16[128,384]{1,0:T(8,128)(2,1)S(1)}, bf16[128,384]{1,0:T(8,128)(2,1)S(1)}, u32[]{:S(2)}, u32[]{:S(2)}) collective-permute-start(bf16[128,384]{1,0:T(8,128)(2,1)S(1)} %maximum_select_fusion.23), channel_id=1, source_target_pairs={{0,2},{1,3},{2,0},{3,1},{4,6},{5,7},{6,4},{7,5},{8,10},{9,11},{10,... | collective-permute-start | bytes 294920 | tf_op jit(solution)/shard_map/ppermute | solution.py:50
  583.2 8.0 %collective-permute-start.21 = (bf16[128,384]{1,0:T(8,128)(2,1)S(1)}, bf16[128,384]{1,0:T(8,128)(2,1)S(1)}, u32[]{:S(2)}, u32[]{:S(2)}) collective-permute-start(bf16[128,384]{1,0:T(8,128)(2,1)S(1)} %maximum_select_fusion.22), channel_id=1, source_target_pairs={{0,8},{1,9},{2,10},{3,11},{4,12},{5,13},{6,14},{7,15},{8,0},{9,1},... | collective-permute-start | bytes 294920 | tf_op jit(solution)/shard_map/ppermute | solution.py:50
  584.3 4.8 collective-permute-start.11
  586.3 11.5 %collective-permute-start.52 = (bf16[128,384]{1,0:T(8,128)(2,1)S(1)}, bf16[128,384]{1,0:T(8,128)(2,1)S(1)}, u32[]{:S(2)}, u32[]{:S(2)}) collective-permute-start(bf16[128,384]{1,0:T(8,128)(2,1)S(1)} %maximum_select_fusion.25), channel_id=1, source_target_pairs={{0,6},{1,7},{2,4},{3,5},{4,2},{5,3},{6,0},{7,1},{8,14},{9,15},{10,... | collective-permute-start | bytes 294920 | tf_op jit(solution)/shard_map/ppermute | solution.py:50
  589.1 5.8 collective-permute-start.12
  591.0 13.3 %collective-permute-start.42 = (bf16[256,384]{1,0:T(8,128)(2,1)S(1)}, bf16[256,384]{1,0:T(8,128)(2,1)S(1)}, u32[]{:S(2)}, u32[]{:S(2)}) collective-permute-start(bf16[256,384]{1,0:T(8,128)(2,1)S(1)} %maximum_select_fusion.19), channel_id=1, source_target_pairs={{0,2},{1,3},{2,0},{3,1},{4,6},{5,7},{6,4},{7,5},{8,10},{9,11},{10,... | collective-permute-start | bytes 589832 | tf_op jit(solution)/shard_map/ppermute | solution.py:50
  591.3 8.0 %collective-permute-start.22 = (bf16[256,384]{1,0:T(8,128)(2,1)S(1)}, bf16[256,384]{1,0:T(8,128)(2,1)S(1)}, u32[]{:S(2)}, u32[]{:S(2)}) collective-permute-start(bf16[256,384]{1,0:T(8,128)(2,1)S(1)} %maximum_select_fusion.17), channel_id=1, source_target_pairs={{0,48},{1,49},{2,50},{3,51},{4,52},{5,53},{6,54},{7,55},{8,56},{9,... | collective-permute-start | bytes 589832 | tf_op jit(solution)/shard_map/ppermute | solution.py:50
  595.1 8.8 %collective-permute-start.13 = (bf16[512,384]{1,0:T(8,128)(2,1)S(1)}, bf16[512,384]{1,0:T(8,128)(2,1)S(1)}, u32[]{:S(2)}, u32[]{:S(2)}) collective-permute-start(bf16[512,384]{1,0:T(8,128)(2,1)S(1)} %maximum_select_fusion.11), channel_id=1, source_target_pairs={{0,16},{1,17},{2,18},{3,19},{4,20},{5,21},{6,22},{7,23},{8,24},{9,... | collective-permute-start | bytes 1179656 | tf_op jit(solution)/shard_map/ppermute | solution.py:50
  595.4 6.1 collective-permute-start.32
  597.9 9.0 %collective-permute-start.53 = (bf16[256,384]{1,0:T(8,128)(2,1)S(1)}, bf16[256,384]{1,0:T(8,128)(2,1)S(1)}, u32[]{:S(2)}, u32[]{:S(2)}) collective-permute-start(bf16[256,384]{1,0:T(8,128)(2,1)S(1)} %maximum_select_fusion.20), channel_id=1, source_target_pairs={{0,16},{1,17},{2,18},{3,19},{4,20},{5,21},{6,22},{7,23},{8,24},{9,... | collective-permute-start | bytes 589832 | tf_op jit(solution)/shard_map/ppermute | solution.py:50
  599.4 10.2 %collective-permute-start.23 = (bf16[512,384]{1,0:T(8,128)(2,1)S(1)}, bf16[512,384]{1,0:T(8,128)(2,1)S(1)}, u32[]{:S(2)}, u32[]{:S(2)}) collective-permute-start(bf16[512,384]{1,0:T(8,128)(2,1)S(1)} %maximum_select_fusion.12), channel_id=1, source_target_pairs={{0,6},{1,7},{2,4},{3,5},{4,2},{5,3},{6,0},{7,1},{8,14},{9,15},{10,... | collective-permute-start | bytes 1179656 | tf_op jit(solution)/shard_map/ppermute | solution.py:50
  601.7 10.0 %collective-permute-start.33 = (bf16[512,384]{1,0:T(8,128)(2,1)S(1)}, bf16[512,384]{1,0:T(8,128)(2,1)S(1)}, u32[]{:S(2)}, u32[]{:S(2)}) collective-permute-start(bf16[512,384]{1,0:T(8,128)(2,1)S(1)} %maximum_select_fusion.13), channel_id=1, source_target_pairs={{0,48},{1,49},{2,50},{3,51},{4,52},{5,53},{6,54},{7,55},{8,56},{9,... | collective-permute-start | bytes 1179656 | tf_op jit(solution)/shard_map/ppermute | solution.py:50
  604.2 18.1 %collective-permute-start.14 = (bf16[1024,384]{1,0:T(8,128)(2,1)S(1)}, bf16[1024,384]{1,0:T(8,128)(2,1)S(1)}, u32[]{:S(2)}, u32[]{:S(2)}) collective-permute-start(bf16[1024,384]{1,0:T(8,128)(2,1)S(1)} %maximum_select_fusion.6), channel_id=1, source_target_pairs={{0,2},{1,3},{2,0},{3,1},{4,6},{5,7},{6,4},{7,5},{8,10},{9,11},{10,... | collective-permute-start | bytes 2359304 | tf_op jit(solution)/shard_map/ppermute | solution.py:50
  604.5 9.4 %collective-permute-start.43 = (bf16[512,384]{1,0:T(8,128)(2,1)S(1)}, bf16[512,384]{1,0:T(8,128)(2,1)S(1)}, u32[]{:S(2)}, u32[]{:S(2)}) collective-permute-start(bf16[512,384]{1,0:T(8,128)(2,1)S(1)} %maximum_select_fusion.14), channel_id=1, source_target_pairs={{0,8},{1,9},{2,10},{3,11},{4,12},{5,13},{6,14},{7,15},{8,0},{9,1},... | collective-permute-start | bytes 1179656 | tf_op jit(solution)/shard_map/ppermute | solution.py:50
  607.0 12.7 %collective-permute-start.54 = (bf16[512,384]{1,0:T(8,128)(2,1)S(1)}, bf16[512,384]{1,0:T(8,128)(2,1)S(1)}, u32[]{:S(2)}, u32[]{:S(2)}) collective-permute-start(bf16[512,384]{1,0:T(8,128)(2,1)S(1)} %maximum_select_fusion.15), channel_id=1, source_target_pairs={{0,2},{1,3},{2,0},{3,1},{4,6},{5,7},{6,4},{7,5},{8,10},{9,11},{10,... | collective-permute-start | bytes 1179656 | tf_op jit(solution)/shard_map/ppermute | solution.py:50
  610.0 16.0 %collective-permute-start.24 = (bf16[1024,384]{1,0:T(8,128)(2,1)S(1)}, bf16[1024,384]{1,0:T(8,128)(2,1)S(1)}, u32[]{:S(2)}, u32[]{:S(2)}) collective-permute-start(bf16[1024,384]{1,0:T(8,128)(2,1)S(1)} %maximum_select_fusion.7), channel_id=1, source_target_pairs={{0,16},{1,17},{2,18},{3,19},{4,20},{5,21},{6,22},{7,23},{8,24},{9,... | collective-permute-start | bytes 2359304 | tf_op jit(solution)/shard_map/ppermute | solution.py:50
  612.0 16.6 %collective-permute-start.34 = (bf16[1024,384]{1,0:T(8,128)(2,1)S(1)}, bf16[1024,384]{1,0:T(8,128)(2,1)S(1)}, u32[]{:S(2)}, u32[]{:S(2)}) collective-permute-start(bf16[1024,384]{1,0:T(8,128)(2,1)S(1)} %maximum_select_fusion.8), channel_id=1, source_target_pairs={{0,6},{1,7},{2,4},{3,5},{4,2},{5,3},{6,0},{7,1},{8,14},{9,15},{10,... | collective-permute-start | bytes 2359304 | tf_op jit(solution)/shard_map/ppermute | solution.py:50
  614.2 16.6 %collective-permute-start.44 = (bf16[1024,384]{1,0:T(8,128)(2,1)S(1)}, bf16[1024,384]{1,0:T(8,128)(2,1)S(1)}, u32[]{:S(2)}, u32[]{:S(2)}) collective-permute-start(bf16[1024,384]{1,0:T(8,128)(2,1)S(1)} %maximum_select_fusion.9), channel_id=1, source_target_pairs={{0,48},{1,49},{2,50},{3,51},{4,52},{5,53},{6,54},{7,55},{8,56},{9,... | collective-permute-start | bytes 2359304 | tf_op jit(solution)/shard_map/ppermute | solution.py:50
  620.0 16.6 %collective-permute-start.55 = (bf16[1024,384]{1,0:T(8,128)(2,1)S(1)}, bf16[1024,384]{1,0:T(8,128)(2,1)S(1)}, u32[]{:S(2)}, u32[]{:S(2)}) collective-permute-start(bf16[1024,384]{1,0:T(8,128)(2,1)S(1)} %maximum_select_fusion.10), channel_id=1, source_target_pairs={{0,8},{1,9},{2,10},{3,11},{4,12},{5,13},{6,14},{7,15},{8,0},{9,1},... | collective-permute-start | bytes 2359304 | tf_op jit(solution)/shard_map/ppermute | solution.py:50
  638.2 26.7 %collective-permute-start.56 = (bf16[10240,384]{1,0:T(8,128)(2,1)}, bf16[10240,384]{1,0:T(8,128)(2,1)}, u32[]{:S(2)}, u32[]{:S(2)}) collective-permute-start(bf16[10240,384]{1,0:T(8,128)(2,1)} %fusion.78), channel_id=1, source_target_pairs={{0,1},{1,0},{2,3},{3,2},{4,5},{5,4},{6,7},{7,6},{8,9},{9,8},{10,11... | collective-permute-start | bytes 23592968 | tf_op jit(solution)/shard_map/ppermute | solution.py:50
  (253 other events, 1238.1 us)
